TPU v7x, 32 devices: a whole 2x2x4 slice. The times are simulated.
32 devices in a mesh: rep: 4 (over y, x), shard: 8 (over z, core).
Axes of the slice: x: 2, y: 2, z: 4, core: 2. Of those that a mesh axis runs over, the one named last changes fastest.
Arguments:
- images: bfloat16 [384, 14, 14, 512], P(('rep', 'shard')), may hold values from -6 to 6
- counts: int32 [32], P(('rep', 'shard')), may hold values from 3 to 12, as said below
- w_qkv: bfloat16 [512, 1536], P('shard'), may hold values from -0.25 to 0.25
- b_qv: bfloat16 [1024], P('shard'), may hold values from -3 to 3
- w_proj: bfloat16 [512, 512], P('shard'), may hold values from -0.75 to 0.75
- b_proj: bfloat16 [512], P('shard'), may hold values from -3 to 3
- w_fc1: bfloat16 [512, 2048], P('shard'), may hold values from -0.25 to 0.25
- b_fc1: bfloat16 [2048], P('shard'), may hold values from -3 to 3
- w_fc2: bfloat16 [2048, 512], P('shard'), may hold values from -0.1875 to 0.1875
- b_fc2: bfloat16 [512], P('shard'), may hold values from -3 to 3
- norm1_gain: bfloat16 [512], P('shard'), may hold values from 0.5 to 1.5
- norm1_shift: bfloat16 [512], P('shard'), may hold values from -2 to 2
- norm2_gain: bfloat16 [512], P('shard'), may hold values from 0.5 to 1.5
- norm2_shift: bfloat16 [512], P('shard'), may hold values from -2 to 2
- bias_table: bfloat16 [169, 16], replicated, may hold values from -3 to 3
- cotangent: bfloat16 [384, 14, 14, 512], P(('rep', 'shard')), may hold values from -6 to 6
Outputs:
- block_out: bfloat16 [384, 14, 14, 512], P(('rep', 'shard'))
- image_grad: float32 [384, 14, 14, 512], P(('rep', 'shard'))
- grad_w_qkv: float32 [512, 1536], P('shard')
- grad_b_qv: float32 [1024], P('shard')
- grad_w_proj: float32 [512, 512], P('shard')
- grad_b_proj: float32 [512], P('shard')
- grad_w_fc1: float32 [512, 2048], P('shard')
- grad_b_fc1: float32 [2048], P('shard')
- grad_w_fc2: float32 [2048, 512], P('shard')
- grad_b_fc2: float32 [512], P('shard')
- grad_norm1_gain: float32 [512], P('shard')
- grad_norm1_shift: float32 [512], P('shard')
- grad_norm2_gain: float32 [512], P('shard')
- grad_norm2_shift: float32 [512], P('shard')
- grad_bias_table: float32 [169, 16], replicated
Inputs may be any that keep to these rules, and one draw needn't show every extreme that they name: counts[j] is the number of live image slots of device j: slots j * 12 to j * 12 + counts[j] - 1 hold images, the others are empty and give zero output and no gradient; some device holds 12.
All inputs are finite; a program needn't handle non-finite values.
Results may differ from a plain program's by a relative error of at most 0.018.
Values may be sent and summed in bfloat16 or wider, within the bound.
A program may use at most 128 MiB of HBM per device.

v0:
```python
import math

import jax
import jax.numpy as jnp
from jax import lax
from jax.sharding import PartitionSpec as P

D = 512
HEADS = 16
SIDE = 14
WIN = 7
SHIFT = 3


def layer_norm(values, gain, shift):
    center = values - jnp.mean(values, axis=-1, keepdims=True)
    scaled = center * lax.rsqrt(jnp.mean(center * center, axis=-1, keepdims=True) + 1e-05)
    return scaled * gain + shift


def exact_gelu(values):
    return jax.nn.gelu(values, approximate=False)


def to_windows(block):
    across = SIDE // WIN
    count = block.shape[0]
    parted = block.reshape(count, across, WIN, across, WIN, D).transpose(0, 1, 3, 2, 4, 5)
    return parted.reshape(count * SIDE * SIDE, D)


def from_windows(window_rows, count):
    across = SIDE // WIN
    parted = window_rows.reshape(count, across, across, WIN, WIN, D).transpose(0, 1, 3, 2, 4, 5)
    return parted.reshape(count, SIDE, SIDE, D)


def geometry():
    across = SIDE // WIN
    local = jnp.arange(WIN * WIN, dtype=jnp.int32)
    row_local = local // WIN
    col_local = local % WIN
    windows = jnp.arange(across * across, dtype=jnp.int32)
    row_pos = (windows // across)[:, None] * WIN + row_local[None, :]
    col_pos = (windows % across)[:, None] * WIN + col_local[None, :]
    row_region = (row_pos >= SIDE - WIN).astype(jnp.int32) + (row_pos >= SIDE - SHIFT).astype(
        jnp.int32
    )
    col_region = (col_pos >= SIDE - WIN).astype(jnp.int32) + (col_pos >= SIDE - SHIFT).astype(
        jnp.int32
    )
    region = row_region * 3 + col_region
    penalty = jnp.where(region[:, :, None] == region[:, None, :], 0.0, -100.0).astype(jnp.float32)
    local_pos = jnp.arange(WIN, dtype=jnp.int32)
    offsets = jnp.arange(2 * WIN - 1, dtype=jnp.int32)
    diff_onehot = (
        local_pos[:, None, None] - local_pos[None, :, None] + WIN - 1 == offsets[None, None, :]
    ).astype(jnp.float32)
    return (penalty, diff_onehot)


def table_to_bias(bias_table, penalty, diff_onehot):
    grid_table = bias_table.reshape(2 * WIN - 1, 2 * WIN - 1, HEADS)
    in_window = jnp.einsum(
        "xza,ywb,abh->hxyzw", diff_onehot, diff_onehot, grid_table, precision=lax.Precision.HIGHEST
    )
    in_window = in_window.reshape(HEADS, WIN * WIN, WIN * WIN)
    return in_window[None] + penalty[:, None]


def bias_to_table(grad_bias, diff_onehot):
    in_window = grad_bias.reshape(HEADS, WIN, WIN, WIN, WIN)
    grid_table = jnp.einsum(
        "hxyzw,xza,ywb->abh", in_window, diff_onehot, diff_onehot, precision=lax.Precision.HIGHEST
    )
    return grid_table.reshape((2 * WIN - 1) * (2 * WIN - 1), HEADS)


def prepare(pieces):
    return (
        pieces[0],
        pieces[1].astype(jnp.float32),
        pieces[2],
        pieces[3].astype(jnp.float32),
        pieces[4],
        pieces[5].astype(jnp.float32),
        pieces[6],
        pieces[7].astype(jnp.float32),
        pieces[8].astype(jnp.float32),
        pieces[9].astype(jnp.float32),
        pieces[10].astype(jnp.float32),
        pieces[11].astype(jnp.float32),
    )


def front_part(image_block, weights, bias_win):
    w_qkv, b_qv = (weights[0], weights[1])
    image_count = image_block.shape[0]
    across = SIDE // WIN
    head_dim = D // HEADS
    heads_shape = (image_count, across * across, WIN * WIN, HEADS, head_dim)
    rolled = to_windows(jnp.roll(image_block, (-SHIFT, -SHIFT), axis=(1, 2))).astype(jnp.float32)
    normed_one, pull_one = jax.vjp(layer_norm, rolled, weights[8], weights[9])
    hidden_one = normed_one.astype(jnp.bfloat16)
    project = jnp.dot(hidden_one, w_qkv, preferred_element_type=jnp.float32)
    query_part = (project[:, :D] + b_qv[:D]).astype(jnp.bfloat16).reshape(heads_shape)
    key_part = project[:, D : 2 * D].astype(jnp.bfloat16).reshape(heads_shape)
    value_part = (project[:, 2 * D :] + b_qv[D:]).astype(jnp.bfloat16).reshape(heads_shape)
    scores = (
        jnp.einsum("nwqhe,nwkhe->nwhqk", query_part, key_part, preferred_element_type=jnp.float32)
        * head_dim ** (-0.5)
        + bias_win[None]
    )
    return (rolled, pull_one, hidden_one, query_part, key_part, value_part, scores)


def middle_part(rolled, soft_probs, value_part, weights):
    rows_all = rolled.shape[0]
    probs_low = soft_probs.astype(jnp.bfloat16)
    attended = (
        jnp.einsum("nwhqk,nwkhe->nwqhe", probs_low, value_part, preferred_element_type=jnp.float32)
        .reshape(rows_all, D)
        .astype(jnp.bfloat16)
    )
    residual = rolled + (
        jnp.dot(attended, weights[2], preferred_element_type=jnp.float32) + weights[3]
    )
    normed_two, pull_two = jax.vjp(layer_norm, residual, weights[10], weights[11])
    hidden_two = normed_two.astype(jnp.bfloat16)
    pre_act = jnp.dot(hidden_two, weights[4], preferred_element_type=jnp.float32) + weights[5]
    gelu_values, pull_gelu = jax.vjp(exact_gelu, pre_act)
    activated = gelu_values.astype(jnp.bfloat16)
    return (probs_low, attended, residual, pull_two, hidden_two, pull_gelu, activated)


def body(
    images,
    counts,
    w_qkv,
    b_qv,
    w_proj,
    b_proj,
    w_fc1,
    b_fc1,
    w_fc2,
    b_fc2,
    norm1_gain,
    norm1_shift,
    norm2_gain,
    norm2_shift,
    bias_table,
    cotangent,
):
    slot_count = images.shape[0]
    group_images = math.gcd(slot_count, 3)
    block_count = slot_count // group_images
    live_slot = (jnp.arange(slot_count, dtype=jnp.int32) < counts[0])[:, None, None, None]
    penalty, diff_onehot = geometry()
    bias_win = table_to_bias(bias_table.astype(jnp.float32), penalty, diff_onehot)
    weights_fwd = prepare(
        (
            lax.all_gather(w_qkv, "shard", axis=0, tiled=True),
            lax.all_gather(b_qv, "shard", axis=0, tiled=True),
            lax.all_gather(w_proj, "shard", axis=0, tiled=True),
            lax.all_gather(b_proj, "shard", axis=0, tiled=True),
            lax.all_gather(w_fc1, "shard", axis=0, tiled=True),
            lax.all_gather(b_fc1, "shard", axis=0, tiled=True),
            lax.all_gather(w_fc2, "shard", axis=0, tiled=True),
            lax.all_gather(b_fc2, "shard", axis=0, tiled=True),
            lax.all_gather(norm1_gain, "shard", axis=0, tiled=True),
            lax.all_gather(norm1_shift, "shard", axis=0, tiled=True),
            lax.all_gather(norm2_gain, "shard", axis=0, tiled=True),
            lax.all_gather(norm2_shift, "shard", axis=0, tiled=True),
        )
    )
    block_shape = (block_count, group_images, SIDE, SIDE, D)
    image_blocks = images.reshape(block_shape)

    def forward_step(unused_state, image_block):
        rolled, pull_one, hidden_one, query_part, key_part, value_part, scores = front_part(
            image_block, weights_fwd, bias_win
        )
        row_peak = jnp.max(scores, axis=-1, keepdims=True)
        exp_part = jnp.exp(scores - row_peak)
        row_total = jnp.sum(exp_part, axis=-1, keepdims=True)
        soft_probs = exp_part / row_total
        log_total = (row_peak + jnp.log(row_total))[..., 0]
        probs_low, attended, residual, pull_two, hidden_two, pull_gelu, activated = middle_part(
            rolled, soft_probs, value_part, weights_fwd
        )
        output = residual + (
            jnp.dot(activated, weights_fwd[6], preferred_element_type=jnp.float32) + weights_fwd[7]
        )
        output = jnp.roll(from_windows(output, image_block.shape[0]), (SHIFT, SHIFT), axis=(1, 2))
        return (unused_state, (output, log_total))

    unused_final, (outputs, log_totals) = lax.scan(
        forward_step, jnp.zeros((), jnp.int32), image_blocks
    )
    block_out = jnp.where(live_slot, outputs.reshape(images.shape), 0.0).astype(jnp.bfloat16)
    weights_back = prepare(
        (
            lax.all_gather(w_qkv, "shard", axis=0, tiled=True),
            lax.all_gather(b_qv, "shard", axis=0, tiled=True),
            lax.all_gather(w_proj, "shard", axis=0, tiled=True),
            lax.all_gather(b_proj, "shard", axis=0, tiled=True),
            lax.all_gather(w_fc1, "shard", axis=0, tiled=True),
            lax.all_gather(b_fc1, "shard", axis=0, tiled=True),
            lax.all_gather(w_fc2, "shard", axis=0, tiled=True),
            lax.all_gather(b_fc2, "shard", axis=0, tiled=True),
            lax.all_gather(norm1_gain, "shard", axis=0, tiled=True),
            lax.all_gather(norm1_shift, "shard", axis=0, tiled=True),
            lax.all_gather(norm2_gain, "shard", axis=0, tiled=True),
            lax.all_gather(norm2_shift, "shard", axis=0, tiled=True),
        )
    )
    cot_live = jnp.where(live_slot, cotangent, jnp.zeros_like(cotangent)).reshape(block_shape)
    head_scale = (D // HEADS) ** (-0.5)

    def backward_step(totals, inputs):
        image_block, cot_block, log_total = inputs
        rolled, pull_one, hidden_one, query_part, key_part, value_part, scores = front_part(
            image_block, weights_back, bias_win
        )
        soft_probs = jnp.exp(scores - log_total[..., None])
        probs_low, attended, residual, pull_two, hidden_two, pull_gelu, activated = middle_part(
            rolled, soft_probs, value_part, weights_back
        )
        rows_all = rolled.shape[0]
        grad_out = to_windows(jnp.roll(cot_block, (-SHIFT, -SHIFT), axis=(1, 2)))
        grad_w2 = jnp.einsum("tm,td->md", activated, grad_out, preferred_element_type=jnp.float32)
        grad_b2 = jnp.sum(grad_out.astype(jnp.float32), axis=0)
        grad_act = jnp.einsum(
            "td,md->tm", grad_out, weights_back[6], preferred_element_type=jnp.float32
        )
        grad_pre = pull_gelu(grad_act)[0].astype(jnp.bfloat16)
        grad_w1 = jnp.einsum("td,tm->dm", hidden_two, grad_pre, preferred_element_type=jnp.float32)
        grad_b1 = jnp.sum(grad_pre.astype(jnp.float32), axis=0)
        grad_hidden_two = jnp.einsum(
            "tm,dm->td", grad_pre, weights_back[4], preferred_element_type=jnp.float32
        )
        grad_norm_res, grad_gain_two, grad_shift_two = pull_two(grad_hidden_two)
        grad_residual = grad_out.astype(jnp.float32) + grad_norm_res
        grad_branch = grad_residual.astype(jnp.bfloat16)
        grad_wp = jnp.einsum("td,te->de", attended, grad_branch, preferred_element_type=jnp.float32)
        grad_bp = jnp.sum(grad_branch.astype(jnp.float32), axis=0)
        grad_attended = (
            jnp.einsum(
                "te,de->td", grad_branch, weights_back[2], preferred_element_type=jnp.float32
            )
            .astype(jnp.bfloat16)
            .reshape(value_part.shape)
        )
        grad_probs = jnp.einsum(
            "nwqhe,nwkhe->nwhqk", grad_attended, value_part, preferred_element_type=jnp.float32
        )
        grad_value = jnp.einsum(
            "nwhqk,nwqhe->nwkhe", probs_low, grad_attended, preferred_element_type=jnp.float32
        ).astype(jnp.bfloat16)
        row_inner = jnp.sum(soft_probs * grad_probs, axis=-1, keepdims=True)
        grad_scores = (soft_probs * (grad_probs - row_inner)).astype(jnp.bfloat16)
        grad_query = (
            jnp.einsum(
                "nwhqk,nwkhe->nwqhe", grad_scores, key_part, preferred_element_type=jnp.float32
            )
            * head_scale
        ).astype(jnp.bfloat16)
        grad_key = (
            jnp.einsum(
                "nwhqk,nwqhe->nwkhe", grad_scores, query_part, preferred_element_type=jnp.float32
            )
            * head_scale
        ).astype(jnp.bfloat16)
        grad_bias = jnp.sum(grad_scores.astype(jnp.float32), axis=(0, 1))
        query_rows = grad_query.reshape(rows_all, D)
        value_rows = grad_value.reshape(rows_all, D)
        grad_project = jnp.concatenate(
            [query_rows, grad_key.reshape(rows_all, D), value_rows], axis=1
        )
        grad_wqkv = jnp.einsum(
            "td,te->de", hidden_one, grad_project, preferred_element_type=jnp.float32
        )
        grad_bqv = jnp.concatenate(
            [
                jnp.sum(query_rows.astype(jnp.float32), axis=0),
                jnp.sum(value_rows.astype(jnp.float32), axis=0),
            ]
        )
        grad_hidden_one = jnp.einsum(
            "te,de->td", grad_project, weights_back[0], preferred_element_type=jnp.float32
        )
        grad_norm_in, grad_gain_one, grad_shift_one = pull_one(grad_hidden_one)
        grad_rows = grad_residual + grad_norm_in
        image_grad_block = jnp.roll(
            from_windows(grad_rows, image_block.shape[0]), (SHIFT, SHIFT), axis=(1, 2)
        )
        block_terms = (
            grad_wqkv,
            grad_bqv,
            grad_wp,
            grad_bp,
            grad_w1,
            grad_b1,
            grad_w2,
            grad_b2,
            grad_gain_one,
            grad_shift_one,
            grad_gain_two,
            grad_shift_two,
            grad_bias,
        )
        return (jax.tree.map(jnp.add, totals, block_terms), image_grad_block)

    initial = tuple((jnp.zeros(weight_item.shape, jnp.float32) for weight_item in weights_back)) + (
        jnp.zeros((HEADS, WIN * WIN, WIN * WIN), jnp.float32),
    )
    totals, grad_blocks = lax.scan(backward_step, initial, (image_blocks, cot_live, log_totals))
    image_grad = grad_blocks.reshape(images.shape)
    table_local = bias_to_table(totals[12], diff_onehot)
    owned = (
        lax.psum_scatter(
            totals[0].astype(jnp.bfloat16), "shard", scatter_dimension=0, tiled=True
        ).astype(jnp.float32),
        lax.psum_scatter(
            totals[1].astype(jnp.bfloat16), "shard", scatter_dimension=0, tiled=True
        ).astype(jnp.float32),
        lax.psum_scatter(
            totals[2].astype(jnp.bfloat16), "shard", scatter_dimension=0, tiled=True
        ).astype(jnp.float32),
        lax.psum_scatter(
            totals[3].astype(jnp.bfloat16), "shard", scatter_dimension=0, tiled=True
        ).astype(jnp.float32),
        lax.psum_scatter(
            totals[4].astype(jnp.bfloat16), "shard", scatter_dimension=0, tiled=True
        ).astype(jnp.float32),
        lax.psum_scatter(
            totals[5].astype(jnp.bfloat16), "shard", scatter_dimension=0, tiled=True
        ).astype(jnp.float32),
        lax.psum_scatter(
            totals[6].astype(jnp.bfloat16), "shard", scatter_dimension=0, tiled=True
        ).astype(jnp.float32),
        lax.psum_scatter(
            totals[7].astype(jnp.bfloat16), "shard", scatter_dimension=0, tiled=True
        ).astype(jnp.float32),
        lax.psum_scatter(
            totals[8].astype(jnp.bfloat16), "shard", scatter_dimension=0, tiled=True
        ).astype(jnp.float32),
        lax.psum_scatter(
            totals[9].astype(jnp.bfloat16), "shard", scatter_dimension=0, tiled=True
        ).astype(jnp.float32),
        lax.psum_scatter(
            totals[10].astype(jnp.bfloat16), "shard", scatter_dimension=0, tiled=True
        ).astype(jnp.float32),
        lax.psum_scatter(
            totals[11].astype(jnp.bfloat16), "shard", scatter_dimension=0, tiled=True
        ).astype(jnp.float32),
    )
    summed = (
        lax.psum(owned[0].astype(jnp.bfloat16), "rep").astype(jnp.float32),
        lax.psum(owned[1].astype(jnp.bfloat16), "rep").astype(jnp.float32),
        lax.psum(owned[2].astype(jnp.bfloat16), "rep").astype(jnp.float32),
        lax.psum(owned[3].astype(jnp.bfloat16), "rep").astype(jnp.float32),
        lax.psum(owned[4].astype(jnp.bfloat16), "rep").astype(jnp.float32),
        lax.psum(owned[5].astype(jnp.bfloat16), "rep").astype(jnp.float32),
        lax.psum(owned[6].astype(jnp.bfloat16), "rep").astype(jnp.float32),
        lax.psum(owned[7].astype(jnp.bfloat16), "rep").astype(jnp.float32),
        lax.psum(owned[8].astype(jnp.bfloat16), "rep").astype(jnp.float32),
        lax.psum(owned[9].astype(jnp.bfloat16), "rep").astype(jnp.float32),
        lax.psum(owned[10].astype(jnp.bfloat16), "rep").astype(jnp.float32),
        lax.psum(owned[11].astype(jnp.bfloat16), "rep").astype(jnp.float32),
    )
    table_total = lax.psum(table_local, ("rep", "shard"))
    return (
        block_out,
        image_grad,
        summed[0],
        summed[1],
        summed[2],
        summed[3],
        summed[4],
        summed[5],
        summed[6],
        summed[7],
        summed[8],
        summed[9],
        summed[10],
        summed[11],
        table_total,
    )


def solution(mesh):
    in_specs = (
        P(("rep", "shard"), None, None, None),
        P(("rep", "shard")),
        P("shard", None),
        P("shard"),
        P("shard", None),
        P("shard"),
        P("shard", None),
        P("shard"),
        P("shard", None),
        P("shard"),
        P("shard"),
        P("shard"),
        P("shard"),
        P("shard"),
        P(),
        P(("rep", "shard"), None, None, None),
    )
    out_specs = (
        P(("rep", "shard"), None, None, None),
        P(("rep", "shard"), None, None, None),
        P("shard", None),
        P("shard"),
        P("shard", None),
        P("shard"),
        P("shard", None),
        P("shard"),
        P("shard", None),
        P("shard"),
        P("shard"),
        P("shard"),
        P("shard"),
        P("shard"),
        P(),
    )
    return jax.shard_map(body, mesh=mesh, in_specs=in_specs, out_specs=out_specs, check_vma=False)
```

profile of v0, /device:TPU:0, one launch (start us, length us, event | category | flops | bytes accessed | tf_op | source)
XLA Modules:
  0.0 1144.0 jit_solution(10403402058504349824)
XLA Ops:
  18.0 18.8 %all-reduce.15 = (bf16[512]{0:T(512)(128)(2,1)S(1)}, bf16[512]{0:T(512)(128)(2,1)S(1)}, bf16[512]{0:T(512)(128)(2,1)S(1)}, bf16[512]{0:T(512)(128)(2,1)S(1)}, bf...) all-reduce(bf16[512]{0:T(512)(128)(2,1)S(1)} %dynamic-update-slice, ...), channel_id=1, replica_groups=mesh['rep'=4,'shard'=8] {'shard'}, use_global_device_ids=true, to_apply=%add | all-reduce | flops 3072 | bytes 12288
  36.9 8.6 all-gather
  45.5 10.3 all-gather.1
  62.1 15.4 %all_gather.51 = bf16[512,512]{1,0:T(8,128)(2,1)S(1)} all-gather(bf16[64,512]{1,0:T(8,128)(2,1)S(1)} %copy-done.58), channel_id=1, replica_groups=mesh['rep'=4,'shard'=8] {'shard'}, dimensions={0}, use_global_device_ids=true | all-gather | bytes 589824 | tf_op jit(solution)/shard_map/all_gather | solution.py:164
  77.6 22.4 %all-gather.10.cloned.1.call-done = bf16[2048,512]{1,0:T(8,128)(2,1)} async-done(((bf16[256,512]{1,0:T(8,128)(2,1)}), bf16[2048,512]{1,0:T(8,128)(2,1)}) %all-gather.10.cloned.1.call-update) | async-done | bytes 2097168 | tf_op jit(solution)/shard_map/all_gather | solution.py:168
  100.0 245.8 %while.52 = (s32[]{:T(128)}, bf16[4,3,14,14,512]{4,3,2,1,0:T(8,128)(2,1)}, f32[4,3,4,16,49]{4,3,2,1,0:T(8,128)}, bf16[4,3,14,14,512]{4,3,2,1,0:T(8,128)(2,1)}, f...) while((s32[]{:T(128)}, ...), condition=%wide.region_7.8_spmd.clone.clone, body=%wide.region_0.7_spmd.clone.sunk.clone | while | flops 3856420096 | bytes 67894280 | solution.py:197
  150.7 5.4 fusion.297
  160.5 14.2 %fusion.299 = bf16[588,512]{1,0:T(8,128)(2,1)S(1)} fusion(f32[588,512]{1,0:T(8,128)S(1)} %get-tuple-element.1098, bf16[2048,512]{1,0:T(8,128)(2,1)} %get-tuple-element.1267, bf16[512,2048]{1,0:T(8,128)(2,1)} %get-tuple-element.1265, f32[2048]{0:T(1024)S(1)} %get-tuple-element.1266, f32[512]{0:T(512)S(1)} %get-tuple-element.1268, ...), kind=kOutput, calls=%fused_computation.43.clone.1.clone | convolution fusion | flops 2548137984 | bytes 6019680 | tf_op jit(solution)/shard_map/while/body/eval_jaxpr/dot_general | solution.py:192
  207.1 5.4 fusion.297
  216.9 14.2 %fusion.299 = bf16[588,512]{1,0:T(8,128)(2,1)S(1)} fusion(f32[588,512]{1,0:T(8,128)S(1)} %get-tuple-element.1098, bf16[2048,512]{1,0:T(8,128)(2,1)} %get-tuple-element.1267, bf16[512,2048]{1,0:T(8,128)(2,1)} %get-tuple-element.1265, f32[2048]{0:T(1024)S(1)} %get-tuple-element.1266, f32[512]{0:T(512)S(1)} %get-tuple-element.1268, ...), kind=kOutput, calls=%fused_computation.43.clone.1.clone | convolution fusion | flops 2548137984 | bytes 6019680 | tf_op jit(solution)/shard_map/while/body/eval_jaxpr/dot_general | solution.py:192
  263.5 5.4 fusion.297
  273.3 14.2 %fusion.299 = bf16[588,512]{1,0:T(8,128)(2,1)S(1)} fusion(f32[588,512]{1,0:T(8,128)S(1)} %get-tuple-element.1098, bf16[2048,512]{1,0:T(8,128)(2,1)} %get-tuple-element.1267, bf16[512,2048]{1,0:T(8,128)(2,1)} %get-tuple-element.1265, f32[2048]{0:T(1024)S(1)} %get-tuple-element.1266, f32[512]{0:T(512)S(1)} %get-tuple-element.1268, ...), kind=kOutput, calls=%fused_computation.43.clone.1.clone | convolution fusion | flops 2548137984 | bytes 6019680 | tf_op jit(solution)/shard_map/while/body/eval_jaxpr/dot_general | solution.py:192
  320.0 5.4 fusion.297
  329.8 14.2 %fusion.299 = bf16[588,512]{1,0:T(8,128)(2,1)S(1)} fusion(f32[588,512]{1,0:T(8,128)S(1)} %get-tuple-element.1098, bf16[2048,512]{1,0:T(8,128)(2,1)} %get-tuple-element.1267, bf16[512,2048]{1,0:T(8,128)(2,1)} %get-tuple-element.1265, f32[2048]{0:T(1024)S(1)} %get-tuple-element.1266, f32[512]{0:T(512)S(1)} %get-tuple-element.1268, ...), kind=kOutput, calls=%fused_computation.43.clone.1.clone | convolution fusion | flops 2548137984 | bytes 6019680 | tf_op jit(solution)/shard_map/while/body/eval_jaxpr/dot_general | solution.py:192
  345.8 7.3 broadcast_select_fusion
  353.1 545.8 %while.53 = (s32[]{:T(128)}, f32[512,1536]{1,0:T(8,128)}, f32[1024]{0:T(1024)S(1)}, f32[512,512]{1,0:T(8,128)}, f32[512]{0:T(512)}, /*index=5*/f32[512,2048]{1,0...) while((s32[]{:T(128)}, f32[512,1536]{1,0:T(8,128)}, ...), condition=%wide.region_28.29_spmd.clone.clone, body=%wide.region_8.28_spmd.clone.sunk.clone | while | flops 10184808448 | bytes 387502528 | solution.py:317
  409.4 13.1 %convert_reduce_fusion.18 = (f32[2048]{0:T(1024)S(1)}, bf16[588,2048]{1,0:T(8,128)(2,1)S(1)}, f32[588,2048]{1,0:T(8,128)S(1)}) fusion(f32[588,2048]{1,0:T(8,128)S(1)} %fusion.337, f32[2048]{0:T(1024)S(1)} %copy-done.35, bf16[588,512]{1,0:T(8,128)(2,1)S(1)} %copy-done.9, bf16[2048,512]{1,0:T(8,128)(2,1)S(1)} %copy-done.61), kind=kOutput, calls=%fused_computation.111.clone.1.clone | convolution fusion | flops 1323440128 | bytes 14757888 | tf_op jit(solution)/shard_map/while/body/eval_jaxpr/td,md->tm/dot_general | solution.py:233
  456.0 5.9 multiply_reduce_fusion.28
  544.6 13.4 %convert_reduce_fusion.18 = (f32[2048]{0:T(1024)S(1)}, bf16[588,2048]{1,0:T(8,128)(2,1)S(1)}, f32[588,2048]{1,0:T(8,128)S(1)}) fusion(f32[588,2048]{1,0:T(8,128)S(1)} %fusion.337, f32[2048]{0:T(1024)S(1)} %copy-done.35, bf16[588,512]{1,0:T(8,128)(2,1)S(1)} %copy-done.9, bf16[2048,512]{1,0:T(8,128)(2,1)S(1)} %copy-done.61), kind=kOutput, calls=%fused_computation.111.clone.1.clone | convolution fusion | flops 1323440128 | bytes 14757888 | tf_op jit(solution)/shard_map/while/body/eval_jaxpr/td,md->tm/dot_general | solution.py:233
  591.3 5.9 multiply_reduce_fusion.28
  680.2 13.1 %convert_reduce_fusion.18 = (f32[2048]{0:T(1024)S(1)}, bf16[588,2048]{1,0:T(8,128)(2,1)S(1)}, f32[588,2048]{1,0:T(8,128)S(1)}) fusion(f32[588,2048]{1,0:T(8,128)S(1)} %fusion.337, f32[2048]{0:T(1024)S(1)} %copy-done.35, bf16[588,512]{1,0:T(8,128)(2,1)S(1)} %copy-done.9, bf16[2048,512]{1,0:T(8,128)(2,1)S(1)} %copy-done.61), kind=kOutput, calls=%fused_computation.111.clone.1.clone | convolution fusion | flops 1323440128 | bytes 14757888 | tf_op jit(solution)/shard_map/while/body/eval_jaxpr/td,md->tm/dot_general | solution.py:233
  726.7 5.9 multiply_reduce_fusion.28
  815.5 13.1 %convert_reduce_fusion.18 = (f32[2048]{0:T(1024)S(1)}, bf16[588,2048]{1,0:T(8,128)(2,1)S(1)}, f32[588,2048]{1,0:T(8,128)S(1)}) fusion(f32[588,2048]{1,0:T(8,128)S(1)} %fusion.337, f32[2048]{0:T(1024)S(1)} %copy-done.35, bf16[588,512]{1,0:T(8,128)(2,1)S(1)} %copy-done.9, bf16[2048,512]{1,0:T(8,128)(2,1)S(1)} %copy-done.61), kind=kOutput, calls=%fused_computation.111.clone.1.clone | convolution fusion | flops 1323440128 | bytes 14757888 | tf_op jit(solution)/shard_map/while/body/eval_jaxpr/td,md->tm/dot_general | solution.py:233
  862.2 5.9 multiply_reduce_fusion.28
  912.2 19.5 %reduce-scatter.7.cloned.1.call-done = bf16[64,512]{1,0:T(8,128)(2,1)} async-done(((bf16[512,512]{1,0:T(8,128)(2,1)}), bf16[64,512]{1,0:T(8,128)(2,1)}) %reduce-scatter.7.cloned.1.call-update) | async-done | bytes 65552 | tf_op jit(solution)/shard_map/reduce_scatter | solution.py:327
  931.7 34.6 %reduce-scatter.5.cloned.1.call-done = bf16[64,1536]{1,0:T(8,128)(2,1)} async-done(((bf16[512,1536]{1,0:T(8,128)(2,1)}), bf16[64,1536]{1,0:T(8,128)(2,1)}) %reduce-scatter.5.cloned.1.call-update) | async-done | bytes 196624 | tf_op jit(solution)/shard_map/reduce_scatter | solution.py:321
  966.3 36.0 %reduce-scatter.9.cloned.1.call-done = bf16[64,2048]{1,0:T(8,128)(2,1)} async-done(((bf16[512,2048]{1,0:T(8,128)(2,1)}), bf16[64,2048]{1,0:T(8,128)(2,1)}) %reduce-scatter.9.cloned.1.call-update) | async-done | bytes 262160 | tf_op jit(solution)/shard_map/reduce_scatter | solution.py:333
  1002.3 37.0 %reduce-scatter.11.cloned.1.call-done = bf16[256,512]{1,0:T(8,128)(2,1)} async-done(((bf16[2048,512]{1,0:T(8,128)(2,1)}), bf16[256,512]{1,0:T(8,128)(2,1)}) %reduce-scatter.11.cloned.1.call-update) | async-done | bytes 262160 | tf_op jit(solution)/shard_map/reduce_scatter | solution.py:339
  1042.1 26.9 %all-reduce.14 = (bf16[1024]{0:T(1024)(128)(2,1)S(1)}, bf16[512]{0:T(512)(128)(2,1)S(1)}, bf16[2048]{0:T(1024)(128)(2,1)S(1)}, bf16[512]{0:T(512)(128)(2,1)S(1)}...) all-reduce(bf16[1024]{0:T(1024)(128)(2,1)S(1)} %convert_element_typ, ...), channel_id=3, replica_groups=mesh['rep'=4,'shard'=8] {'shard'}, use_global_device_ids=true, to_apply=%region_31.32.clone | all-reduce | flops 6144 | bytes 24576
  1069.5 9.8 all-reduce.16
  1086.0 5.4 copy.135
  1093.2 36.9 %psum.103 = f32[169,16]{0,1:T(8,128)} all-reduce(f32[169,16]{0,1:T(8,128)S(1)} %reshape.489), channel_id=1, replica_groups=mesh['rep'=4,'shard'=8] {'rep','shard'}, use_global_device_ids=true, to_apply=%region_53.54 | all-reduce | flops 2704 | bytes 21632 | tf_op jit(solution)/shard_map/psum | solution.py:372
  (1088 shorter events, 650.9 us)
Async XLA Ops:
  7.2 70.4 %all-gather.6.cloned.1.call-start = ((), (), s32[]{:S(2)}) async-start(), calls=%async_computation.4 | async-start | bytes 1769472 | tf_op jit(solution)/shard_map/all_gather | solution.py:162
  7.9 69.7 %all-gather.8.cloned.1.call-start = ((), (), s32[]{:S(2)}) async-start(), calls=%async_computation.5 | async-start | bytes 2359296 | tf_op jit(solution)/shard_map/all_gather | solution.py:166
  8.7 91.3 %all-gather.10.cloned.1.call-start = ((), (), s32[]{:S(2)}) async-start(), calls=%async_computation.6 | async-start | bytes 2359296 | tf_op jit(solution)/shard_map/all_gather | solution.py:168
  9.4 922.3 %reduce-scatter.7.cloned.1.call-start = ((), (), s32[]{:S(2)}) async-start(), calls=%async_computation.8 | async-start | bytes 589824 | tf_op jit(solution)/shard_map/reduce_scatter | solution.py:327
  100.0 245.8 %copy-start.59 = (pred[12]{0:T(512)(128)(4,1)S(1)}, pred[12]{0:T(512)(128)(4,1)}, u32[]{:S(2)}) copy-start(pred[12]{0:T(512)(128)(4,1)} %iota_compare_fusion.1) | copy-start | bytes 40
  345.8 7.4 copy-start.37
  345.8 7.4 copy-start.38
  361.0 44.2 %copy-start.2 = (f32[588,512]{1,0:T(8,128)}, f32[588,512]{1,0:T(8,128)S(1)}, u32[]{:S(2)}) copy-start(f32[588,512]{1,0:T(8,128)S(1)} %reshape.623) | copy-start | bytes 3612676 | tf_op jit(solution)/shard_map/while
  409.4 13.1 %copy-start.13 = (f32[2048,512]{1,0:T(8,128)S(1)}, f32[2048,512]{1,0:T(8,128)}, u32[]{:S(2)}) copy-start(f32[2048,512]{1,0:T(8,128)} %get-tuple-element.1309) | copy-start | bytes 12582916 | tf_op jit(solution)/shard_map/while
  434.5 6.1 copy-start.56
  456.0 6.0 slice-start
  496.2 44.3 %copy-start.2 = (f32[588,512]{1,0:T(8,128)}, f32[588,512]{1,0:T(8,128)S(1)}, u32[]{:S(2)}) copy-start(f32[588,512]{1,0:T(8,128)S(1)} %reshape.623) | copy-start | bytes 3612676 | tf_op jit(solution)/shard_map/while
  544.6 13.4 %copy-start.13 = (f32[2048,512]{1,0:T(8,128)S(1)}, f32[2048,512]{1,0:T(8,128)}, u32[]{:S(2)}) copy-start(f32[2048,512]{1,0:T(8,128)} %get-tuple-element.1309) | copy-start | bytes 12582916 | tf_op jit(solution)/shard_map/while
  570.1 6.1 copy-start.56
  591.3 6.0 slice-start
  631.6 44.5 %copy-start.2 = (f32[588,512]{1,0:T(8,128)}, f32[588,512]{1,0:T(8,128)S(1)}, u32[]{:S(2)}) copy-start(f32[588,512]{1,0:T(8,128)S(1)} %reshape.623) | copy-start | bytes 3612676 | tf_op jit(solution)/shard_map/while
  680.2 13.1 %copy-start.13 = (f32[2048,512]{1,0:T(8,128)S(1)}, f32[2048,512]{1,0:T(8,128)}, u32[]{:S(2)}) copy-start(f32[2048,512]{1,0:T(8,128)} %get-tuple-element.1309) | copy-start | bytes 12582916 | tf_op jit(solution)/shard_map/while
  705.3 6.1 copy-start.56
  767.2 44.2 %copy-start.2 = (f32[588,512]{1,0:T(8,128)}, f32[588,512]{1,0:T(8,128)S(1)}, u32[]{:S(2)}) copy-start(f32[588,512]{1,0:T(8,128)S(1)} %reshape.623) | copy-start | bytes 3612676 | tf_op jit(solution)/shard_map/while
  815.5 13.1 %copy-start.13 = (f32[2048,512]{1,0:T(8,128)S(1)}, f32[2048,512]{1,0:T(8,128)}, u32[]{:S(2)}) copy-start(f32[2048,512]{1,0:T(8,128)} %get-tuple-element.1309) | copy-start | bytes 12582916 | tf_op jit(solution)/shard_map/while
  840.7 6.1 copy-start.56
  862.1 6.0 slice-start
  901.1 65.3 %reduce-scatter.5.cloned.1.call-start = ((), (), s32[]{:S(2)}) async-start(), calls=%async_computation.7 | async-start | bytes 1769472 | tf_op jit(solution)/shard_map/reduce_scatter | solution.py:321
  904.4 97.9 %reduce-scatter.9.cloned.1.call-start = ((), (), s32[]{:S(2)}) async-start(), calls=%async_computation.9 | async-start | bytes 2359296 | tf_op jit(solution)/shard_map/reduce_scatter | solution.py:333
  908.3 131.0 %reduce-scatter.11.cloned.1.call-start = ((), (), s32[]{:S(2)}) async-start(), calls=%async_computation.10 | async-start | bytes 2359296 | tf_op jit(solution)/shard_map/reduce_scatter | solution.py:339
  912.1 129.1 %copy-start.57 = (f32[512]{0:T(512)S(1)}, f32[512]{0:T(512)}, u32[]{:S(2)}) copy-start(f32[512]{0:T(512)} %get-tuple-element.274) | copy-start | bytes 6148
  912.1 129.8 %copy-start.54 = (f32[512]{0:T(512)S(1)}, f32[512]{0:T(512)}, u32[]{:S(2)}) copy-start(f32[512]{0:T(512)} %get-tuple-element.279) | copy-start | bytes 6148
  912.1 129.8 %copy-start.51 = (f32[512]{0:T(512)S(1)}, f32[512]{0:T(512)}, u32[]{:S(2)}) copy-start(f32[512]{0:T(512)} %get-tuple-element.280) | copy-start | bytes 6148
  912.1 129.9 %copy-start.48 = (f32[512]{0:T(512)S(1)}, f32[512]{0:T(512)}, u32[]{:S(2)}) copy-start(f32[512]{0:T(512)} %get-tuple-element.281) | copy-start | bytes 6148
  912.1 129.9 %copy-start.45 = (f32[512]{0:T(512)S(1)}, f32[512]{0:T(512)}, u32[]{:S(2)}) copy-start(f32[512]{0:T(512)} %get-tuple-element.282) | copy-start | bytes 6148
  912.1 171.3 %copy-start.25 = (f32[16,49,49]{1,2,0:T(8,128)S(1)}, f32[16,49,49]{1,2,0:T(8,128)}, u32[]{:S(2)}) copy-start(f32[16,49,49]{1,2,0:T(8,128)} %get-tuple-element.283) | copy-start | bytes 460996
  912.2 217.9 %all-reduce.20.cloned.1.call-start = ((), (), s32[]{:S(2)}) async-start(), calls=%async_computation.11 | async-start | bytes 1572864 | tf_op jit(solution)/shard_map/psum | solution.py:359
  (200 other events, 497.9 us)
Sparse Core Ops, SparseCore 0:
  9.7 28.3 all-gather.5
  39.6 30.1 all-gather.7
  71.4 28.5 all-gather.9
  901.2 30.4 reduce-scatter.6
  934.0 32.3 reduce-scatter.4
  968.6 33.6 reduce-scatter.8
  1004.7 34.5 reduce-scatter.10
  1043.0 48.0 all-reduce.19
where the time goes:
time: 1160 us; the launch traced here: 1140 us
  local copies, waits for them, and re-layouts  376 us (32%)
  matrix products  329 us (28%)
  waiting for transfers between devices  152 us (13%)
  blocking collectives  127 us (11%)
  other arithmetic  111 us (10%)
  loops' own time  31.1 us (3%)
  between operations  18.1 us (2%)
    dot_general x4, matrix products, forward_step(): jnp.dot(activated, weights_fwd[6], preferred_element_type=jnp.float32)  56.8 us
    while x432, local copies, waits for them, and re-layouts  55 us
    dot_general x4, matrix products, backward_step(): jnp.einsum('td,md->tm', grad_out, weights_back[6], preferred_element_type...  52.6 us
    reshape x12, local copies, waits for them, and re-layouts, front_part(): (project[:, :D] + b_qv[:D]).astype(jnp.bfloat16).reshape(heads_shape)  51.3 us
    reshape x12, local copies, waits for them, and re-layouts, front_part(): key_part = project[:, D:2 * D].astype(jnp.bfloat16).reshape(heads_shape)  50.1 us
    unnamed x2, blocking collectives  45.7 us
    reshape x12, local copies, waits for them, and re-layouts, front_part(): (project[:, 2 * D:] + b_qv[D:]).astype(jnp.bfloat16).reshape(heads_shape)  45.3 us
    reduce_scatter x1, waiting for transfers between devices, body(): lax.psum_scatter(totals[6].astype(jnp.bfloat16), 'shard', scatter_dimensi...  37 us
  transfers between devices with their start and end apart: 8, of which 5 were waited for; matrix products, arithmetic and copies ran while one was open for 3% of the time, Pallas kernels for 0%

commit v1 on v0

v1 whole, which is shorter than its diff:
```python
import numpy as np

import jax
import jax.numpy as jnp
from jax import lax
from jax.experimental import pallas as pl
from jax.experimental.pallas import tpu as pltpu
from jax.sharding import PartitionSpec as P

D = 512
HEADS = 16
MLP = 2048
SIDE = 14
WIN = 7
SHIFT = 3
TABLE = 169
ROWS = 256
SCALE = (D // HEADS) ** -0.5
BF = jnp.bfloat16
F32 = jnp.float32


def place_matrix():
    place = np.zeros((ROWS, SIDE * 16), np.float32)
    for win in range(4):
        for tok in range(WIN * WIN):
            row = ((win // 2) * WIN + tok // WIN + SHIFT) % SIDE
            col = ((win % 2) * WIN + tok % WIN + SHIFT) % SIDE
            place[win * 64 + tok, row * 16 + col] = 1.0
    return place


def head_mask():
    rows, lanes = np.arange(512)[:, None], np.arange(256)[None, :]
    return (rows // 64 == lanes // 32).astype(np.float32)


def rel_index():
    tok = np.arange(WIN * WIN)
    r, c = tok // WIN, tok % WIN
    rel = (r[None, :] - r[:, None] + 6) * 13 + (c[None, :] - c[:, None] + 6)
    full = np.full((64, 64), -1)
    full[:49, :49] = rel
    return full.reshape(-1)


def penalty_term():
    out = np.zeros((4, 1, 64, 1, 64), np.float32)
    tok = np.arange(WIN * WIN)
    for win in range(4):
        row = (win // 2) * WIN + tok // WIN
        col = (win % 2) * WIN + tok % WIN
        reg = ((row >= 7) * 1 + (row >= 11)) * 3 + (col >= 7) * 1 + (col >= 11)
        out[win, 0, :49, 0, :49] = np.where(reg[:, None] == reg[None, :], 0.0, -100.0)
        out[win, 0, 49:] = -1e30
    return out


def nn(a, b):
    return jnp.dot(a, b, preferred_element_type=F32)


def nt(a, b):
    return lax.dot_general(a, b, (((1,), (1,)), ((), ())), preferred_element_type=F32)


def tn(a, b):
    return lax.dot_general(a, b, (((0,), (0,)), ((), ())), preferred_element_type=F32)


def norm_parts(x):
    center = x - jnp.mean(x, axis=-1, keepdims=True)
    inv = lax.rsqrt(jnp.mean(center * center, axis=-1, keepdims=True) + 1e-05)
    return center * inv, inv


def spread(block, mask):
    return jnp.concatenate([block] * 8, axis=0) * mask


def fold(full, mask):
    total = full[0:64] * mask[0:64]
    for h in range(1, 8):
        total += full[64 * h : 64 * h + 64] * mask[64 * h : 64 * h + 64]
    return total


def colsum(x):
    return jnp.sum(x, axis=0, keepdims=True)


def front_kernel(
    cnt, img, cot, place, mask, bias, w, bq, bv, gain, shift, xw_o, cw_o, qkv_o, pt_o, att_o, scr
):
    step = pl.program_id(0)

    @pl.when(step == 0)
    def _():
        scr[...] = jnp.zeros_like(scr)

    for r in range(SIDE):
        scr[pl.ds(16 * r, SIDE), :] = img[0, r]
    xw = nn(place[...], scr[...])
    xw_o[...] = xw.astype(BF)
    live = (step < cnt[0]).astype(F32)
    for r in range(SIDE):
        scr[pl.ds(16 * r, SIDE), :] = cot[0, r]
    cw_o[...] = (nn(place[...], scr[...]) * live).astype(BF)
    xhat, _ = norm_parts(xw)
    hidden = (xhat * gain[...] + shift[...]).astype(BF)
    qkv_o[:, :D] = (nn(hidden, w[:, :D]) + bq[...]).astype(BF)
    qkv_o[:, D : 2 * D] = nn(hidden, w[:, D : 2 * D]).astype(BF)
    qkv_o[:, 2 * D :] = (nn(hidden, w[:, 2 * D :]) + bv[...]).astype(BF)
    mask_low = mask[...]
    for win in range(4):
        rows = slice(64 * win, 64 * win + 64)
        for g in range(2):
            lo = 256 * g
            qb = spread(qkv_o[rows, lo : lo + 256], mask_low)
            st = nt(qkv_o[rows, D + lo : D + lo + 256], qb) * SCALE + bias[win, g]
            e = jnp.exp(st - jnp.max(st, axis=0, keepdims=True))
            p = (e / jnp.sum(e, axis=0, keepdims=True)).astype(BF)
            pt_o[0, win, g] = p
            full = tn(p, qkv_o[rows, 2 * D + lo : 2 * D + lo + 256])
            att_o[rows, lo : lo + 256] = fold(full, mask_low.astype(F32)).astype(BF)


def mlp_kernel(
    cnt, xw, cw, att, unplace, wp, w1, w2, bp, b1, b2, gain, shift,
    out_o, gr_o, ga_o, dwp_o, dw1_o, dw2_o, gbp, gb1, gb2, gg, gs,
    awp, aw1, aw2,
):
    step = pl.program_id(0)

    @pl.when(step == 0)
    def _():
        for ref in (awp, aw1, aw2, gbp, gb1, gb2, gg, gs):
            ref[...] = jnp.zeros_like(ref)

    res = xw[...].astype(F32) + (nn(att[...], wp[...]) + bp[...])
    xhat, inv = norm_parts(res)
    hidden = (xhat * gain[...] + shift[...]).astype(BF)
    g_low = cw[...]
    ff = jnp.zeros_like(res)
    gh = jnp.zeros_like(res)
    for j in range(4):
        cols = slice(512 * j, 512 * j + 512)
        pre = nn(hidden, w1[:, cols]) + b1[:, cols]
        half = 0.5 * (1.0 + lax.erf(pre * 0.7071067811865476))
        act = (pre * half).astype(BF)
        ff += nn(act, w2[cols, :])
        slope = half + pre * jnp.exp(-0.5 * pre * pre) * 0.3989422804014327
        gp32 = nt(g_low, w2[cols, :]) * slope
        gp = gp32.astype(BF)
        aw2[:, cols] += tn(g_low, act)
        aw1[:, cols] += tn(hidden, gp)
        gb1[:, cols] += colsum(gp.astype(F32))
        gh += nt(gp, w1[:, cols])
    out = res + (ff + b2[...])
    for i in range(2):
        live = (2 * step + i < cnt[0]).astype(F32)
        low = (out[ROWS * i : ROWS * i + ROWS] * live).astype(BF)
        back = nn(unplace[...], low).astype(BF)
        for r in range(SIDE):
            out_o[i, r] = back[16 * r : 16 * r + SIDE]
    g32 = g_low.astype(F32)
    gb2[...] += colsum(g32)
    gg[...] += colsum(gh * xhat)
    gs[...] += colsum(gh)
    e = gh * gain[...]
    gr = g32 + inv * (
        e - jnp.mean(e, axis=-1, keepdims=True) - xhat * jnp.mean(e * xhat, axis=-1, keepdims=True)
    )
    gr_o[...] = gr
    br = gr.astype(BF)
    gbp[...] += colsum(br.astype(F32))
    awp[...] += tn(att[...], br)
    ga_o[...] = nt(br, wp[...]).astype(BF)

    @pl.when(step == pl.num_programs(0) - 1)
    def _():
        dwp_o[...] = awp[...].astype(BF)
        dw1_o[...] = aw1[...].astype(BF)
        dw2_o[...] = aw2[...].astype(BF)


def back_kernel(
    xw, qkv, pt, ga, gr, unplace, mask, w, gain, shift,
    ig_o, dw_o, gbq, gbv, gg, gs, gbias, aw, gproj,
):
    step = pl.program_id(0)

    @pl.when(step == 0)
    def _():
        for ref in (aw, gbq, gbv, gg, gs, gbias):
            ref[...] = jnp.zeros_like(ref)

    mask_low = mask[...]
    for win in range(4):
        rows = slice(64 * win, 64 * win + 64)
        for g in range(2):
            lo = 256 * g
            db = spread(ga[rows, lo : lo + 256], mask_low)
            qb = spread(qkv[rows, lo : lo + 256], mask_low)
            p_low = pt[0, win, g]
            p = p_low.astype(F32)
            dp = nt(qkv[rows, 2 * D + lo : 2 * D + lo + 256], db)
            ds = (p * (dp - jnp.sum(p * dp, axis=0, keepdims=True))).astype(BF)
            gbias[g] += ds.astype(F32)
            gproj[rows, 2 * D + lo : 2 * D + lo + 256] = nn(p_low, db).astype(BF)
            gproj[rows, D + lo : D + lo + 256] = (nn(ds, qb) * SCALE).astype(BF)
            full = tn(ds, qkv[rows, D + lo : D + lo + 256])
            gproj[rows, lo : lo + 256] = (fold(full, mask_low.astype(F32)) * SCALE).astype(BF)
    gbq[...] += colsum(gproj[:, :D].astype(F32))
    gbv[...] += colsum(gproj[:, 2 * D :].astype(F32))
    xhat, inv = norm_parts(xw[...].astype(F32))
    hidden = (xhat * gain[...] + shift[...]).astype(BF)
    aw[...] += tn(hidden, gproj[...])
    gh = nt(gproj[...], w[...])
    gg[...] += colsum(gh * xhat)
    gs[...] += colsum(gh)
    e = gh * gain[...]
    grad = gr[...] + inv * (
        e - jnp.mean(e, axis=-1, keepdims=True) - xhat * jnp.mean(e * xhat, axis=-1, keepdims=True)
    )
    high = grad.astype(BF)
    low = (grad - high.astype(F32)).astype(BF)
    back = nn(unplace[...], high) + nn(unplace[...], low)
    for r in range(SIDE):
        ig_o[0, r] = back[16 * r : 16 * r + SIDE]

    @pl.when(step == pl.num_programs(0) - 1)
    def _():
        dw_o[...] = aw[...].astype(BF)


def whole(shape):
    return pl.BlockSpec(shape, lambda i: (0,) * len(shape))


def params():
    return pltpu.CompilerParams(
        dimension_semantics=("arbitrary",), vmem_limit_bytes=56 * 1024 * 1024
    )


def sds(shape, dtype):
    return jax.ShapeDtypeStruct(shape, dtype)


def body(
    images, counts, w_qkv, b_qv, w_proj, b_proj, w_fc1, b_fc1, w_fc2, b_fc2,
    norm1_gain, norm1_shift, norm2_gain, norm2_shift, bias_table, cotangent,
):
    n = images.shape[0]
    shards = lax.axis_size("shard")
    me = lax.axis_index("shard")
    vecs = (b_qv, b_proj, b_fc1, b_fc2, norm1_gain, norm1_shift, norm2_gain, norm2_shift)
    sizes = [v.shape[0] for v in vecs]
    packed = lax.all_gather(jnp.concatenate(vecs), "shard", axis=0).astype(F32)
    gw_qkv = lax.all_gather(w_qkv, "shard", axis=0, tiled=True)
    gw_proj = lax.all_gather(w_proj, "shard", axis=0, tiled=True)
    gw_fc1 = lax.all_gather(w_fc1, "shard", axis=0, tiled=True)
    gw_fc2 = lax.all_gather(w_fc2, "shard", axis=0, tiled=True)
    full, at = [], 0
    for size in sizes:
        full.append(packed[:, at : at + size].reshape(1, size * shards))
        at += size
    bqv, bp, b1, b2, g1, s1, g2, s2 = full

    place = place_matrix()
    place_in = jnp.asarray(place, BF)
    place_out = jnp.asarray(place.T, BF)
    mask = jnp.asarray(head_mask(), BF)
    rel = jnp.asarray(rel_index(), jnp.int32)
    onehot = (jnp.arange(TABLE, dtype=jnp.int32)[:, None] == rel[None, :]).astype(BF)
    bias = lax.dot_general(
        bias_table, onehot, (((0,), (0,)), ((), ())), preferred_element_type=F32
    ).reshape(2, 8, 64, 64).transpose(0, 2, 1, 3)
    bias = (bias[None] + jnp.asarray(penalty_term())).reshape(4, 2, 64, 512)

    smem = pl.BlockSpec(memory_space=pltpu.SMEM)
    image_spec = pl.BlockSpec((1, SIDE, SIDE, D), lambda i: (i, 0, 0, 0))
    rows = lambda count, width: pl.BlockSpec((count, width), lambda i: (i, 0))
    probs_spec = pl.BlockSpec((1, 4, 2, 64, 512), lambda i: (i, 0, 0, 0, 0))
    vec = whole((1, D))
    total = n * ROWS

    xw, cw, qkv, pt, att = pl.pallas_call(
        front_kernel,
        grid=(n,),
        in_specs=[
            smem, image_spec, image_spec, whole((ROWS, 224)), whole((512, 256)),
            whole((4, 2, 64, 512)), whole((D, 3 * D)), vec, vec, vec, vec,
        ],
        out_specs=[rows(ROWS, D), rows(ROWS, D), rows(ROWS, 3 * D), probs_spec, rows(ROWS, D)],
        out_shape=[
            sds((total, D), BF), sds((total, D), BF), sds((total, 3 * D), BF),
            sds((n, 4, 2, 64, 512), BF), sds((total, D), BF),
        ],
        scratch_shapes=[pltpu.VMEM((224, D), BF)],
        compiler_params=params(),
        cost_estimate=pl.CostEstimate(
            flops=60_000_000_000, bytes_accessed=30_000_000, transcendentals=0
        ),
        name="front",
    )(
        counts, images, cotangent, place_in, mask, bias, gw_qkv,
        bqv[:, :D], bqv[:, D:], g1, s1,
    )

    wide = whole((1, MLP))
    block_out, gr, ga, dwp, dw1, dw2t, gbp, gb1, gb2, gg2, gs2 = pl.pallas_call(
        mlp_kernel,
        grid=(n // 2,),
        in_specs=[
            smem, rows(512, D), rows(512, D), rows(512, D), whole((224, ROWS)),
            whole((D, D)), whole((D, MLP)), whole((MLP, D)), vec, wide, vec, vec, vec,
        ],
        out_specs=[
            pl.BlockSpec((2, SIDE, SIDE, D), lambda i: (i, 0, 0, 0)),
            rows(512, D), rows(512, D), whole((D, D)), whole((D, MLP)), whole((D, MLP)),
            vec, wide, vec, vec, vec,
        ],
        out_shape=[
            sds(images.shape, BF), sds((total, D), F32), sds((total, D), BF),
            sds((D, D), BF), sds((D, MLP), BF), sds((D, MLP), BF),
            sds((1, D), F32), sds((1, MLP), F32), sds((1, D), F32), sds((1, D), F32),
            sds((1, D), F32),
        ],
        scratch_shapes=[
            pltpu.VMEM((D, D), F32), pltpu.VMEM((D, MLP), F32), pltpu.VMEM((D, MLP), F32),
        ],
        compiler_params=params(),
        cost_estimate=pl.CostEstimate(
            flops=60_000_000_000, bytes_accessed=30_000_000, transcendentals=0
        ),
        name="mlp",
    )(counts, xw, cw, att, place_out, gw_proj, gw_fc1, gw_fc2, bp, b1, b2, g2, s2)

    def scatter(term):
        return lax.psum_scatter(term, "shard", scatter_dimension=0, tiled=True)

    own_mlp = (scatter(dwp), scatter(dw1), scatter(dw2t.T))

    image_grad, dwq, gbq, gbv, gg1, gs1, gbias = pl.pallas_call(
        back_kernel,
        grid=(n,),
        in_specs=[
            rows(ROWS, D), rows(ROWS, 3 * D), probs_spec, rows(ROWS, D), rows(ROWS, D),
            whole((224, ROWS)), whole((512, 256)), whole((D, 3 * D)), vec, vec,
        ],
        out_specs=[
            image_spec, whole((D, 3 * D)), vec, vec, vec, vec, whole((2, 64, 512)),
        ],
        out_shape=[
            sds(images.shape, F32), sds((D, 3 * D), BF), sds((1, D), F32), sds((1, D), F32),
            sds((1, D), F32), sds((1, D), F32), sds((2, 64, 512), F32),
        ],
        scratch_shapes=[pltpu.VMEM((D, 3 * D), F32), pltpu.VMEM((ROWS, 3 * D), BF)],
        compiler_params=params(),
        cost_estimate=pl.CostEstimate(
            flops=80_000_000_000, bytes_accessed=30_000_000, transcendentals=0
        ),
        name="back",
    )(xw, qkv, pt, ga, gr, place_out, mask, gw_qkv, g1, s1)

    own = (scatter(dwq),) + own_mlp
    own = [lax.psum(term, "rep").astype(F32) for term in own]
    by_head = gbias.reshape(2, 64, 8, 64).transpose(0, 2, 1, 3).reshape(HEADS, 4096)
    table = lax.dot_general(
        onehot.astype(F32), by_head, (((1,), (1,)), ((), ())),
        precision=lax.Precision.HIGHEST, preferred_element_type=F32,
    )
    terms = (jnp.concatenate([gbq, gbv], axis=1), gbp, gb1, gb2, gg1, gs1, gg2, gs2)
    flat = jnp.concatenate([t.reshape(-1) for t in terms] + [table.reshape(-1)])
    flat = lax.psum(flat, ("rep", "shard"))
    small, at = [], 0
    for size in sizes:
        small.append(lax.dynamic_slice_in_dim(flat, at + me * size, size))
        at += size * shards
    table = flat[at:].reshape(TABLE, HEADS)
    return (
        block_out, image_grad, own[0], small[0], own[1], small[1], own[2], small[2],
        own[3], small[3], small[4], small[5], small[6], small[7], table,
    )


def solution(mesh):
    img = P(("rep", "shard"), None, None, None)
    row, vec = P("shard", None), P("shard")
    weights = (row, vec, row, vec, row, vec, row, vec, vec, vec, vec, vec)
    return jax.shard_map(
        body,
        mesh=mesh,
        in_specs=(img, P(("rep", "shard"))) + weights + (P(), img),
        out_specs=(img, img) + weights + (P(),),
        check_vma=False,
    )
```

time: 1160 us -> 391 us (0.34); the launches traced: 1140 us -> 390 us
  local copies, waits for them, and re-layouts: 376 us -> 16.8 us
  matrix products: 329 us -> 2.68 us
  Pallas kernels: 0 us -> 152 us
  other arithmetic: 111 us -> 6.1 us
  blocking collectives: 127 us -> 71.1 us
  loops' own time: 31.1 us -> 0 us
  waiting for transfers between devices: 152 us -> 126 us
    dot_general x92 -> x2, matrix products: 329 us -> 2.68 us  [the longest x1 1.4 us: body(): lax.dot_general(onehot.astype(F32), by_head, (((1,), (1,)), ((), ())), pr...]
    reshape x85 -> x12, local copies, waits for them, and re-layouts: 221 us -> 4.74 us  [the longest x6 3.93 us: body(): full.append(packed[:, at:at + size].reshape(1, size * shards))]
    pallas_call x0 -> x3, Pallas kernels: none -> 152 us  [the longest x1 62.1 us: body(): pl.pallas_call(mlp_kernel, grid=(n // 2,), in_specs=[smem, rows(512, D),...]
    convert_element_type x52 -> x0, local copies, waits for them, and re-layouts: 63.8 us -> none  [the longest x16 31.2 us: middle_part(): attended = jnp.einsum('nwhqk,nwkhe->nwqhe', probs_low, value_part, prefer...]
    while x432 -> x0, local copies, waits for them, and re-layouts: 55 us -> none
    unnamed x2 -> x0, blocking collectives: 45.7 us -> none
    convert_element_type x48 -> x3, other arithmetic: 36.5 us -> 4.98 us  [body(): own = [lax.psum(term, 'rep').astype(F32) for term in own]]
    another operation x2 -> x0, loops' own time: 31.1 us -> none  [the longest x1 20.8 us: body(): lax.scan(forward_step, jnp.zeros((), jnp.int32), image_blocks)]
  transfers between devices with their start and end apart: 8 -> 8, of which waited for: 5 -> 5; matrix products, arithmetic and copies ran while one was open for 3% -> 5% of each run, Pallas kernels for 0% -> 23%
where the time goes in v1:
time: 391 us; the launch traced here: 390 us
  Pallas kernels  152 us (39%)
  waiting for transfers between devices  126 us (32%)
  blocking collectives  71.1 us (18%)
  local copies, waits for them, and re-layouts  16.8 us (4%)
  between operations  15.2 us (4%)
  other arithmetic  6.1 us (2%)
    reduce_scatter x4, waiting for transfers between devices, scatter(): return lax.psum_scatter(term, 'shard', scatter_dimension=0, tiled=True)  103 us
    pallas_call x1, Pallas kernels, body(): pl.pallas_call(mlp_kernel, grid=(n // 2,), in_specs=[smem, rows(512, D),...  62.1 us
    pallas_call x1, Pallas kernels, body(): pl.pallas_call(back_kernel, grid=(n,), in_specs=[rows(ROWS, D), rows(ROWS...  55 us
    psum x1, blocking collectives, body(): flat = lax.psum(flat, ('rep', 'shard'))  38.2 us
    pallas_call x1, Pallas kernels, body(): pl.pallas_call(front_kernel, grid=(n,), in_specs=[smem, image_spec, image...  34.4 us
    all_gather x1, blocking collectives, body(): gw_proj = lax.all_gather(w_proj, 'shard', axis=0, tiled=True)  17.2 us
    all_gather x1, blocking collectives, body(): packed = lax.all_gather(jnp.concatenate(vecs), 'shard', axis=0).astype(F32)  15.7 us
    psum x1, waiting for transfers between devices, body(): own = [lax.psum(term, 'rep').astype(F32) for term in own]  11.2 us
  transfers between devices with their start and end apart: 8, of which 5 were waited for; matrix products, arithmetic and copies ran while one was open for 5% of the time, Pallas kernels for 23%

profile of v1, /device:TPU:0, one launch (start us, length us, event | category | flops | bytes accessed | tf_op | source)
XLA Modules:
  0.0 390.1 jit_solution(7430825552086725224)
XLA Ops:
  7.3 0.7 all-gather.6.cloned.1.call-update
  8.0 0.7 all-gather.10.cloned.1.call-update
  8.7 0.7 all-gather.8.cloned.1.call-update
  9.5 5.4 %concatenate.9 = bf16[768]{0:T(1024)(128)(2,1)S(1)} concatenate(bf16[128]{0:T(256)(128)(2,1)} %param.24, bf16[64]{0:T(256)(128)(2,1)} %param.26, bf16[256]{0:T(256)(128)(2,1)} %param.28, bf16[64]{0:T(256)(128)(2,1)} %param.30, bf16[64]{0:T(256)(128)(2,1)} %param.31, bf16[64]{0:T(256)(128)(2,1)} %param.32, bf16[64]{0:T(256)(128)(2,1)} %param.33, bf16[64]{0:T(256)(128)(2,1)} %param.34), dimensions={0} | concatenate | bytes 3072 | tf_op jit(solution)/shard_map/concatenate | solution.py:260
  14.9 15.7 %all-gather.1 = bf16[8,1,768]{2,1,0:T(2,128)(2,1)S(1)} all-gather(bf16[1,1,768]{2,1,0:T(2,128)(2,1)S(1)} %reshape.130), channel_id=2, replica_groups=mesh['rep'=4,'shard'=8] {'shard'}, dimensions={0}, use_global_device_ids=true | all-gather | bytes 13824 | tf_op jit(solution)/shard_map/all_gather | solution.py:260
  30.7 0.7 reshape.109.gain
  31.4 0.7 reshape.110.shift
  33.3 1.3 convolution_bitcast_fusion
  35.6 0.6 reshape.111.bp
  36.3 0.7 reshape.113.b2
  36.9 0.6 reshape.114.gain
  37.6 0.7 reshape.115.shift
  38.2 0.6 copy.50
  38.9 17.2 %all_gather.21.wp = bf16[512,512]{1,0:T(8,128)(2,1)} all-gather(bf16[64,512]{1,0:T(8,128)(2,1)S(1)} %copy-done.4), channel_id=1, replica_groups=mesh['rep'=4,'shard'=8] {'shard'}, dimensions={0}, use_global_device_ids=true | all-gather | bytes 589824 | tf_op jit(solution)/shard_map/all_gather | solution.py:262
  56.1 1.1 broadcast_add_fusion.bias
  57.2 34.4 %front.1 = (bf16[3072,512]{1,0:T(8,128)(2,1)}, bf16[3072,512]{1,0:T(8,128)(2,1)}, bf16[3072,1536]{1,0:T(8,128)(2,1)}, bf16[12,4,2,64,512]{4,3,2,1,0:T(8,128)(2,1)}, bf16[3072,512]{1,0:T(8,128)(2,1)}) custom-call(s32[1]{0:T(128)S(6)} %copy.67.cnt, bf16[12,14,14,512]{3,2,1,0:T(8,128)(2,1)} %img.1, bf16[12,14,14,512]{3,2,1,0:T(8,128)(2,1)} %cot.1, ...), custom_call_target="tpu_custom_call" | custom-call | flops 60000002048 | bytes 30000000 | tf_op jit(solution)/shard_map/front/pallas_call | solution.py:289
  91.6 8.2 %all-gather.8.cloned.1.call-done.w1 = bf16[512,2048]{1,0:T(8,128)(2,1)} async-done(((bf16[64,2048]{1,0:T(8,128)(2,1)}), bf16[512,2048]{1,0:T(8,128)(2,1)}) %all-gather.8.cloned.1.call-update) | async-done | bytes 2097168 | tf_op jit(solution)/shard_map/all_gather | solution.py:263
  99.8 62.1 %mlp.1 = (bf16[12,14,14,512]{3,2,1,0:T(8,128)(2,1)}, f32[3072,512]{1,0:T(8,128)}, bf16[3072,512]{1,0:T(8,128)(2,1)}, bf16[512,512]{1,0:T(8,128)(2,1)}, bf16[512,...) custom-call(s32[1]{0:T(128)S(6)} %copy.67.cnt, ...), custom_call_target="tpu_custom_call" | custom-call | flops 60000002048 | bytes 30000000 | tf_op jit(solution)/shard_map/mlp/pallas_call | solution.py:313
  162.3 55.0 %back.1 = (f32[12,14,14,512]{3,2,1,0:T(8,128)}, bf16[512,1536]{1,0:T(8,128)(2,1)}, f32[1,512]{1,0:T(1,128)}, f32[1,512]{1,0:T(1,128)}, f32[1,512]{1,0:T(1,128)},...) custom-call(bf16[3072,512]{1,0:T(8,128)(2,1)} %get-tuple-element.38.xw, bf16[3072,1536]{1,0:T(8,128)(2,1)} %get-tuple-element.42.qkv, ...), custom_call_target="tpu_custom_call" | custom-call | flops 80000000000 | bytes 30000000 | tf_op jit(solution)/shard_map/back/pallas_call | solution.py:346
  218.0 0.7 reduce-scatter.9.cloned.1.call-update
  219.2 1.4 fusion
  220.8 30.5 %reduce-scatter.5.cloned.1.call-done = bf16[64,1536]{1,0:T(8,128)(2,1)} async-done(((bf16[512,1536]{1,0:T(8,128)(2,1)}), bf16[64,1536]{1,0:T(8,128)(2,1)}) %reduce-scatter.5.cloned.1.call-update) | async-done | bytes 196624 | tf_op jit(solution)/shard_map/reduce_scatter | solution.py:342
  251.3 36.1 %reduce-scatter.11.cloned.1.call-done = bf16[256,512]{0,1:T(8,128)(2,1)} async-done(((bf16[2048,512]{0,1:T(8,128)(2,1)}), bf16[256,512]{0,1:T(8,128)(2,1)}) %reduce-scatter.11.cloned.1.call-update) | async-done | bytes 262160 | tf_op jit(solution)/shard_map/reduce_scatter | solution.py:342
  287.4 36.9 %reduce-scatter.9.cloned.1.call-done = bf16[64,2048]{1,0:T(8,128)(2,1)} async-done(((bf16[512,2048]{1,0:T(8,128)(2,1)}), bf16[64,2048]{1,0:T(8,128)(2,1)}) %reduce-scatter.9.cloned.1.call-update) | async-done | bytes 262160 | tf_op jit(solution)/shard_map/reduce_scatter | solution.py:342
  324.4 38.2 %psum.36 = f32[8848]{0:T(1024)S(1)} all-reduce(f32[8848]{0:T(1024)S(1)} %constant_dynamic-update-slice_fusion), channel_id=1, replica_groups=mesh['rep'=4,'shard'=8] {'rep','shard'}, use_global_device_ids=true, to_apply=%region_2.0 | all-reduce | flops 8848 | bytes 70784 | tf_op jit(solution)/shard_map/psum | solution.py:377
  362.7 0.7 copy.47
  363.4 0.6 dynamic_slice.26
  365.2 11.2 %all-reduce.3.cloned.1.call-done = (bf16[256,512]{0,1:T(8,128)(2,1)}, bf16[64,1536]{1,0:T(8,128)(2,1)}, bf16[64,512]{1,0:T(8,128)(2,1)}, bf16[64,2048]{1,0:T(8,128)(2,1)}) async-done(((bf16[256,512]{0,1:T(8,128)(2,1)}, bf16[64,1536]{1,0:T(8,128)(2,1)}, bf16[64,512]{1,0:T(8,128)(2,1)}, bf16[64,2048]{1,0:T(8,128)(2,1)}), (bf16[256,512]{0,1:T(8,128)(2,1)}, bf16[64,1536]{1,0:T(8,128)(2,1)}, ...) | async-done | bytes 786448 | tf_op jit(solution)/shard_map/psum | solution.py:369
  376.4 1.8 convert_element_type.20
  378.2 1.9 copy.46
  380.1 1.7 convert_element_type.18
  381.8 1.5 convert_element_type.19
  (74 shorter events, 4.8 us)
Async XLA Ops:
  7.2 26.1 %copy-start = (bf16[169,16]{0,1:T(8,128)(2,1)S(1)}, bf16[169,16]{0,1:T(8,128)(2,1)}, u32[]{:S(2)}) copy-start(bf16[169,16]{0,1:T(8,128)(2,1)} %param.35) | copy-start | bytes 16228
  7.2 28.1 %copy-start.3 = (f32[4,64,64]{2,1,0:T(8,128)S(1)}, f32[4,64,64]{2,1,0:T(8,128)}, u32[]{:S(2)}) copy-start(f32[4,64,64]{2,1,0:T(8,128)} %constant.60) | copy-start | bytes 196612
  7.2 50.0 %all-gather.6.cloned.1.call-start = ((), (), s32[]{:S(2)}) async-start(), calls=%async_computation.4 | async-start | bytes 1769472 | tf_op jit(solution)/shard_map/all_gather | solution.py:261
  7.9 83.7 %all-gather.10.cloned.1.call-start = ((), (), s32[]{:S(2)}) async-start(), calls=%async_computation.6 | async-start | bytes 2359296 | tf_op jit(solution)/shard_map/all_gather | solution.py:264
  8.7 91.1 %all-gather.8.cloned.1.call-start = ((), (), s32[]{:S(2)}) async-start(), calls=%async_computation.5 | async-start | bytes 2359296 | tf_op jit(solution)/shard_map/all_gather | solution.py:263
  9.4 211.4 %reduce-scatter.7.cloned.1.call-start = ((), (), s32[]{:S(2)}) async-start(), calls=%async_computation.8 | async-start | bytes 589824 | tf_op jit(solution)/shard_map/reduce_scatter | solution.py:342
  34.6 4.3 %copy-start.4 = (bf16[64,512]{1,0:T(8,128)(2,1)S(1)}, bf16[64,512]{1,0:T(8,128)(2,1)}, u32[]{:S(2)}) copy-start(bf16[64,512]{1,0:T(8,128)(2,1)} %param.25) | copy-start | bytes 196612
  162.0 89.3 %reduce-scatter.5.cloned.1.call-start = ((), (), s32[]{:S(2)}) async-start(), calls=%async_computation.7 | async-start | bytes 1769472 | tf_op jit(solution)/shard_map/reduce_scatter | solution.py:342
  217.2 1.5 copy-start.2
  217.3 70.1 %reduce-scatter.11.cloned.1.call-start = ((), (), s32[]{:S(2)}) async-start(), calls=%async_computation.10 | async-start | bytes 2359296 | tf_op jit(solution)/shard_map/reduce_scatter | solution.py:342
  217.9 1.3 copy-start.14
  217.9 106.4 %reduce-scatter.9.cloned.1.call-start = ((), (), s32[]{:S(2)}) async-start(), calls=%async_computation.9 | async-start | bytes 2359296 | tf_op jit(solution)/shard_map/reduce_scatter | solution.py:342
  217.9 2.8 copy-start.12
  217.9 2.8 copy-start.13
  217.9 2.8 copy-start.11
  218.0 2.8 copy-start.5
  218.6 105.7 %copy-start.8 = (f32[1,512]{1,0:T(1,128)S(1)}, f32[1,512]{1,0:T(1,128)}, u32[]{:S(2)}) copy-start(f32[1,512]{1,0:T(1,128)} %get-tuple-element.52) | copy-start | bytes 6148
  218.6 105.7 %copy-start.10 = (f32[1,512]{1,0:T(1,128)S(1)}, f32[1,512]{1,0:T(1,128)}, u32[]{:S(2)}) copy-start(f32[1,512]{1,0:T(1,128)} %get-tuple-element.53) | copy-start | bytes 6148
  218.6 105.7 %copy-start.9 = (f32[1,512]{1,0:T(1,128)S(1)}, f32[1,512]{1,0:T(1,128)}, u32[]{:S(2)}) copy-start(f32[1,512]{1,0:T(1,128)} %get-tuple-element.54) | copy-start | bytes 6148
  218.7 105.7 %copy-start.7 = (f32[1,512]{1,0:T(1,128)S(1)}, f32[1,512]{1,0:T(1,128)}, u32[]{:S(2)}) copy-start(f32[1,512]{1,0:T(1,128)} %get-tuple-element.55) | copy-start | bytes 6148
  218.7 105.7 %copy-start.6 = (f32[1,512]{1,0:T(1,128)S(1)}, f32[1,512]{1,0:T(1,128)}, u32[]{:S(2)}) copy-start(f32[1,512]{1,0:T(1,128)} %get-tuple-element.56) | copy-start | bytes 6148
  218.7 157.7 %all-reduce.3.cloned.1.call-start = ((), (), s32[]{:S(2)}) async-start(), calls=%async_computation.11 | async-start | bytes 1572864 | tf_op jit(solution)/shard_map/psum | solution.py:369
  219.0 164.3 %copy-start.1 = (bf16[169,16]{0,1:T(8,128)(2,1)S(1)}, bf16[169,16]{0,1:T(8,128)(2,1)}, u32[]{:S(2)}) copy-start(bf16[169,16]{0,1:T(8,128)(2,1)} %param.35) | copy-start | bytes 16228
Sparse Core Ops, SparseCore 0:
  9.7 27.8 all-gather.5
  39.2 30.2 all-gather.9
  71.1 28.6 all-gather.7
  162.1 30.3 reduce-scatter.6
  217.4 33.8 reduce-scatter.4
  253.5 33.7 reduce-scatter.10
  289.8 34.4 reduce-scatter.8
  328.0 48.3 all-reduce.2

commit v2 on v1

--- a/solution.py
+++ b/solution.py
@@ -108,9 +108,9 @@
     cw_o[...] = (nn(place[...], scr[...]) * live).astype(BF)
     xhat, _ = norm_parts(xw)
     hidden = (xhat * gain[...] + shift[...]).astype(BF)
-    qkv_o[:, :D] = (nn(hidden, w[:, :D]) + bq[...]).astype(BF)
-    qkv_o[:, D : 2 * D] = nn(hidden, w[:, D : 2 * D]).astype(BF)
-    qkv_o[:, 2 * D :] = (nn(hidden, w[:, 2 * D :]) + bv[...]).astype(BF)
+    qkv_o[:, :D] = (nn(hidden, w[:, :, :D].reshape(D, D)) + bq[...]).astype(BF)
+    qkv_o[:, D : 2 * D] = nn(hidden, w[:, :, D : 2 * D].reshape(D, D)).astype(BF)
+    qkv_o[:, 2 * D :] = (nn(hidden, w[:, :, 2 * D :].reshape(D, D)) + bv[...]).astype(BF)
     mask_low = mask[...]
     for win in range(4):
         rows = slice(64 * win, 64 * win + 64)
@@ -180,8 +180,10 @@
     @pl.when(step == pl.num_programs(0) - 1)
     def _():
         dwp_o[...] = awp[...].astype(BF)
-        dw1_o[...] = aw1[...].astype(BF)
-        dw2_o[...] = aw2[...].astype(BF)
+        for j in range(4):
+            cols = slice(512 * j, 512 * j + 512)
+            dw1_o[j] = aw1[:, cols].astype(BF)
+            dw2_o[cols, :] = aw2[:, cols].T.astype(BF)
 
 
 def back_kernel(
@@ -216,7 +218,7 @@
     xhat, inv = norm_parts(xw[...].astype(F32))
     hidden = (xhat * gain[...] + shift[...]).astype(BF)
     aw[...] += tn(hidden, gproj[...])
-    gh = nt(gproj[...], w[...])
+    gh = nt(gproj[...], w[...].reshape(D, 3 * D))
     gg[...] += colsum(gh * xhat)
     gs[...] += colsum(gh)
     e = gh * gain[...]
@@ -257,15 +259,17 @@
     me = lax.axis_index("shard")
     vecs = (b_qv, b_proj, b_fc1, b_fc2, norm1_gain, norm1_shift, norm2_gain, norm2_shift)
     sizes = [v.shape[0] for v in vecs]
-    packed = lax.all_gather(jnp.concatenate(vecs), "shard", axis=0).astype(F32)
-    gw_qkv = lax.all_gather(w_qkv, "shard", axis=0, tiled=True)
-    gw_proj = lax.all_gather(w_proj, "shard", axis=0, tiled=True)
-    gw_fc1 = lax.all_gather(w_fc1, "shard", axis=0, tiled=True)
+    reps = lax.axis_size("rep")
+    depth = w_qkv.shape[0]
+    extra = [jnp.pad(v[None], ((0, 0), (0, 3 * D - v.shape[0]))) for v in vecs]
+    extra.append(jnp.zeros((8, 3 * D), BF))
+    first = lax.all_gather(jnp.concatenate([w_qkv] + extra, axis=0), "shard", axis=0)
+    second = lax.all_gather(
+        jnp.concatenate([w_fc1, w_proj], axis=1), "shard", axis=0, tiled=True
+    )
     gw_fc2 = lax.all_gather(w_fc2, "shard", axis=0, tiled=True)
-    full, at = [], 0
-    for size in sizes:
-        full.append(packed[:, at : at + size].reshape(1, size * shards))
-        at += size
+    packed = first[:, depth : depth + 8].astype(F32)
+    full = [packed[:, i, :size].reshape(1, size * shards) for i, size in enumerate(sizes)]
     bqv, bp, b1, b2, g1, s1, g2, s2 = full
 
     place = place_matrix()
@@ -291,7 +295,7 @@
         grid=(n,),
         in_specs=[
             smem, image_spec, image_spec, whole((ROWS, 224)), whole((512, 256)),
-            whole((4, 2, 64, 512)), whole((D, 3 * D)), vec, vec, vec, vec,
+            whole((4, 2, 64, 512)), whole((shards, depth, 3 * D)), vec, vec, vec, vec,
         ],
         out_specs=[rows(ROWS, D), rows(ROWS, D), rows(ROWS, 3 * D), probs_spec, rows(ROWS, D)],
         out_shape=[
@@ -305,26 +309,27 @@
         ),
         name="front",
     )(
-        counts, images, cotangent, place_in, mask, bias, gw_qkv,
+        counts, images, cotangent, place_in, mask, bias, first,
         bqv[:, :D], bqv[:, D:], g1, s1,
     )
 
     wide = whole((1, MLP))
-    block_out, gr, ga, dwp, dw1, dw2t, gbp, gb1, gb2, gg2, gs2 = pl.pallas_call(
+    block_out, gr, ga, dwp, dw1, dw2, gbp, gb1, gb2, gg2, gs2 = pl.pallas_call(
         mlp_kernel,
         grid=(n // 2,),
         in_specs=[
             smem, rows(512, D), rows(512, D), rows(512, D), whole((224, ROWS)),
-            whole((D, D)), whole((D, MLP)), whole((MLP, D)), vec, wide, vec, vec, vec,
+            pl.BlockSpec((D, D), lambda i: (0, 4)), whole((D, MLP)), whole((MLP, D)),
+            vec, wide, vec, vec, vec,
         ],
         out_specs=[
             pl.BlockSpec((2, SIDE, SIDE, D), lambda i: (i, 0, 0, 0)),
-            rows(512, D), rows(512, D), whole((D, D)), whole((D, MLP)), whole((D, MLP)),
+            rows(512, D), rows(512, D), whole((D, D)), whole((4, D, D)), whole((MLP, D)),
             vec, wide, vec, vec, vec,
         ],
         out_shape=[
             sds(images.shape, BF), sds((total, D), F32), sds((total, D), BF),
-            sds((D, D), BF), sds((D, MLP), BF), sds((D, MLP), BF),
+            sds((D, D), BF), sds((4, D, D), BF), sds((MLP, D), BF),
             sds((1, D), F32), sds((1, MLP), F32), sds((1, D), F32), sds((1, D), F32),
             sds((1, D), F32),
         ],
@@ -336,19 +341,27 @@
             flops=60_000_000_000, bytes_accessed=30_000_000, transcendentals=0
         ),
         name="mlp",
-    )(counts, xw, cw, att, place_out, gw_proj, gw_fc1, gw_fc2, bp, b1, b2, g2, s2)
-
-    def scatter(term):
-        return lax.psum_scatter(term, "shard", scatter_dimension=0, tiled=True)
-
-    own_mlp = (scatter(dwp), scatter(dw1), scatter(dw2t.T))
+    )(counts, xw, cw, att, place_out, second, second, gw_fc2, bp, b1, b2, g2, s2)
+
+    both = ("rep", "shard")
+    deep = D // (shards * reps)
+    split = lambda term: term.reshape(shards, reps, -1, term.shape[-1]).swapaxes(0, 1)
+    cut = dw1.reshape(4, shards, reps, deep, D).transpose(2, 1, 0, 3, 4)
+    joined = jnp.concatenate(
+        [split(dw2), split(dwp), cut.reshape(reps, shards, 4 * deep, D)], axis=2
+    ).reshape(-1, D)
+    part_mlp = lax.psum_scatter(joined, both, scatter_dimension=0, tiled=True)
+    own_mlp = lax.all_gather(part_mlp, "rep", axis=0)
+    own_two = own_mlp[:, : 4 * deep].reshape(-1, D)
+    own_proj = own_mlp[:, 4 * deep : 5 * deep].reshape(-1, D)
+    own_one = own_mlp[:, 5 * deep :].reshape(reps, 4, deep, D).swapaxes(1, 2).reshape(-1, MLP)
 
     image_grad, dwq, gbq, gbv, gg1, gs1, gbias = pl.pallas_call(
         back_kernel,
         grid=(n,),
         in_specs=[
             rows(ROWS, D), rows(ROWS, 3 * D), probs_spec, rows(ROWS, D), rows(ROWS, D),
-            whole((224, ROWS)), whole((512, 256)), whole((D, 3 * D)), vec, vec,
+            whole((224, ROWS)), whole((512, 256)), whole((shards, depth, 3 * D)), vec, vec,
         ],
         out_specs=[
             image_spec, whole((D, 3 * D)), vec, vec, vec, vec, whole((2, 64, 512)),
@@ -363,10 +376,13 @@
             flops=80_000_000_000, bytes_accessed=30_000_000, transcendentals=0
         ),
         name="back",
-    )(xw, qkv, pt, ga, gr, place_out, mask, gw_qkv, g1, s1)
-
-    own = (scatter(dwq),) + own_mlp
-    own = [lax.psum(term, "rep").astype(F32) for term in own]
+    )(xw, qkv, pt, ga, gr, place_out, mask, first, g1, s1)
+
+    part_qkv = lax.psum_scatter(
+        split(dwq).reshape(-1, 3 * D), both, scatter_dimension=0, tiled=True
+    )
+    own_qkv = lax.all_gather(part_qkv, "rep", axis=0, tiled=True)
+    own = [term.astype(F32) for term in (own_qkv, own_proj, own_one, own_two)]
     by_head = gbias.reshape(2, 64, 8, 64).transpose(0, 2, 1, 3).reshape(HEADS, 4096)
     table = lax.dot_general(
         onehot.astype(F32), by_head, (((1,), (1,)), ((), ())),

time: 391 us -> 461 us (1.18)
  waiting for transfers between devices: 126 us -> 197 us
  blocking collectives: 71.1 us -> 59.7 us
  local copies, waits for them, and re-layouts: 16.8 us -> 25.4 us
    reduce_scatter x4 -> x2, waiting for transfers between devices: 103 us -> 147 us  [the longest x1 102 us: body(): part_mlp = lax.psum_scatter(joined, both, scatter_dimension=0, tiled=True)]
    all_gather x2, waiting for transfers between devices: 8.21 us -> 49 us  [the longest x1 24.9 us: body(): lax.all_gather(jnp.concatenate([w_fc1, w_proj], axis=1), 'shard', axis=0,...]
    all_gather x2, blocking collectives: 32.9 us -> 19.9 us  [the longest x1 11.2 us: body(): own_mlp = lax.all_gather(part_mlp, 'rep', axis=0)]
    psum x1 -> x0, waiting for transfers between devices: 11.2 us -> none  [body(): own = [lax.psum(term, 'rep').astype(F32) for term in own]]
    transpose x0 -> x2, local copies, waits for them, and re-layouts: none -> 4.66 us  [the longest x1 2.7 us: body(): term.reshape(shards, reps, -1, term.shape[-1]).swapaxes(0, 1)]
    pad x0 -> x8, local copies, waits for them, and re-layouts: none -> 4.64 us  [body(): extra = [jnp.pad(v[None], ((0, 0), (0, 3 * D - v.shape[0]))) for v in vecs]]
  transfers between devices with their start and end apart: 8 -> 5, of which waited for: 5 -> 4; matrix products, arithmetic and copies ran while one was open for 5% -> 5% of each run, Pallas kernels for 23% -> 8%
where the time goes in v2:
time: 461 us
  waiting for transfers between devices  197 us (43%)
  Pallas kernels  152 us (33%)
  blocking collectives  59.7 us (13%)
  local copies, waits for them, and re-layouts  25.4 us (6%)
  between operations  14.9 us (3%)
  other arithmetic  8.55 us (2%)
    reduce_scatter x1, waiting for transfers between devices, body(): part_mlp = lax.psum_scatter(joined, both, scatter_dimension=0, tiled=True)  102 us
    pallas_call x1, Pallas kernels, body(): pl.pallas_call(mlp_kernel, grid=(n // 2,), in_specs=[smem, rows(512, D),...  62.6 us
    pallas_call x1, Pallas kernels, body(): pl.pallas_call(back_kernel, grid=(n,), in_specs=[rows(ROWS, D), rows(ROWS...  55 us
    reduce_scatter x1, waiting for transfers between devices, body(): lax.psum_scatter(split(dwq).reshape(-1, 3 * D), both, scatter_dimension=0...  45.1 us
    psum x1, blocking collectives, body(): flat = lax.psum(flat, ('rep', 'shard'))  39.8 us
    pallas_call x1, Pallas kernels, body(): pl.pallas_call(front_kernel, grid=(n,), in_specs=[smem, image_spec, image...  34.8 us
    all_gather x1, waiting for transfers between devices, body(): lax.all_gather(jnp.concatenate([w_fc1, w_proj], axis=1), 'shard', axis=0,...  24.9 us
    all_gather x1, waiting for transfers between devices, body(): lax.all_gather(jnp.concatenate([w_qkv] + extra, axis=0), 'shard', axis=0)  24.2 us
  transfers between devices with their start and end apart: 5, of which 4 were waited for; matrix products, arithmetic and copies ran while one was open for 5% of the time, Pallas kernels for 8%

profile of v2, /device:TPU:0, one launch (start us, length us, event | category | flops | bytes accessed | tf_op | source)
XLA Modules:
  0.0 460.6 jit_solution(13047080509953894041)
XLA Ops:
  7.3 0.7 broadcast_in_dim.32
  8.0 0.7 pad.27
  9.9 0.7 pad.31
  10.6 0.7 pad.32
  12.6 2.9 concatenate.15
  15.6 0.7 all-gather.8.cloned.1.call-update
  16.3 1.7 pad_maximum_fusion.1
  18.8 1.3 convolution_bitcast_fusion
  21.1 1.1 broadcast_add_fusion.bias
  22.2 24.2 %all-gather.10.cloned.1.call-done = bf16[640,1536]{1,0:T(8,128)(2,1)} async-done(((bf16[80,1536]{1,0:T(8,128)(2,1)}), bf16[640,1536]{1,0:T(8,128)(2,1)}) %all-gather.10.cloned.1.call-update) | async-done | bytes 1966096 | tf_op jit(solution)/shard_map/all_gather | solution.py:266
  46.4 1.0 slice_convert_fusion
  51.9 0.7 reshape_squeeze.31.shift
  52.5 34.8 %front.1 = (bf16[3072,512]{1,0:T(8,128)(2,1)}, bf16[3072,512]{1,0:T(8,128)(2,1)}, bf16[3072,1536]{1,0:T(8,128)(2,1)}, bf16[12,4,2,64,512]{4,3,2,1,0:T(8,128)(2,1)}, bf16[3072,512]{1,0:T(8,128)(2,1)}) custom-call(s32[1]{0:T(128)S(6)} %copy.65.cnt, bf16[12,14,14,512]{3,2,1,0:T(8,128)(2,1)} %img.1, bf16[12,14,14,512]{3,2,1,0:T(8,128)(2,1)} %cot.1, ...), custom_call_target="tpu_custom_call" | custom-call | flops 60000002048 | bytes 30000000 | tf_op jit(solution)/shard_map/front/pallas_call | solution.py:293
  87.4 24.9 %all-gather.6.cloned.1.call-done.wp.w1 = bf16[512,2560]{1,0:T(8,128)(2,1)} async-done(((bf16[64,2560]{1,0:T(8,128)(2,1)}), bf16[512,2560]{1,0:T(8,128)(2,1)}) %all-gather.6.cloned.1.call-update) | async-done | bytes 2621456 | tf_op jit(solution)/shard_map/all_gather | solution.py:267
  112.3 62.6 %mlp.1 = (bf16[12,14,14,512]{3,2,1,0:T(8,128)(2,1)}, f32[3072,512]{1,0:T(8,128)}, bf16[3072,512]{1,0:T(8,128)(2,1)}, bf16[512,512]{1,0:T(8,128)(2,1)}, bf16[4,51...) custom-call(s32[1]{0:T(128)S(6)} %copy.65.cnt, ...), custom_call_target="tpu_custom_call" | custom-call | flops 60000002048 | bytes 30000000 | tf_op jit(solution)/shard_map/mlp/pallas_call | solution.py:317
  174.8 55.0 %back.1 = (f32[12,14,14,512]{3,2,1,0:T(8,128)}, bf16[512,1536]{1,0:T(8,128)(2,1)}, f32[1,512]{1,0:T(1,128)}, f32[1,512]{1,0:T(1,128)}, f32[1,512]{1,0:T(1,128)},...) custom-call(bf16[3072,512]{1,0:T(8,128)(2,1)} %get-tuple-element.38.xw, bf16[3072,1536]{1,0:T(8,128)(2,1)} %get-tuple-element.42.qkv, ...), custom_call_target="tpu_custom_call" | custom-call | flops 80000000000 | bytes 30000000 | tf_op jit(solution)/shard_map/back/pallas_call | solution.py:359
  229.8 2.7 copy.41
  232.6 2.0 copy.46
  234.9 0.7 copy-done.3
  235.7 2.4 pad_maximum_fusion
  238.3 0.8 copy-done.4
  239.5 1.4 fusion
  241.2 39.8 %psum.7 = f32[8848]{0:T(1024)S(1)} all-reduce(f32[8848]{0:T(1024)S(1)} %constant_dynamic-update-slice_fusion), channel_id=1, replica_groups=mesh['rep'=4,'shard'=8] {'rep','shard'}, use_global_device_ids=true, to_apply=%region_1.2 | all-reduce | flops 8848 | bytes 70784 | tf_op jit(solution)/shard_map/psum | solution.py:393
  281.1 0.7 copy.48
  283.6 45.1 %reduce-scatter.3.cloned.1.call-done = bf16[16,1536]{1,0:T(8,128)(2,1)} async-done(((bf16[512,1536]{1,0:T(8,128)(2,1)}), bf16[16,1536]{1,0:T(8,128)(2,1)}) %reduce-scatter.3.cloned.1.call-update) | async-done | bytes 49168 | tf_op jit(solution)/shard_map/reduce_scatter | solution.py:381
  328.7 8.8 %all_gather.25 = bf16[64,1536]{1,0:T(8,128)(2,1)S(1)} all-gather(bf16[16,1536]{1,0:T(8,128)(2,1)} %reduce-scatter.3.cloned.1.call-done), channel_id=1, replica_groups=mesh['rep'=4,'shard'=8] {'rep'}, dimensions={0}, use_global_device_ids=true | all-gather | bytes 245760 | tf_op jit(solution)/shard_map/all_gather | solution.py:384
  337.5 0.8 convert_element_type.44
  338.3 101.8 %reduce-scatter.5.cloned.1.call-done = bf16[144,512]{1,0:T(8,128)(2,1)} async-done(((bf16[4608,512]{1,0:T(8,128)(2,1)}), bf16[144,512]{1,0:T(8,128)(2,1)}) %reduce-scatter.5.cloned.1.call-update) | async-done | bytes 147472 | tf_op jit(solution)/shard_map/reduce_scatter | solution.py:353
  440.1 11.2 %all-gather.1 = bf16[576,512]{1,0:T(8,128)(2,1)S(1)} all-gather(bf16[144,512]{1,0:T(8,128)(2,1)} %reduce-scatter.5.cloned.1.call-done), channel_id=3, replica_groups=mesh['rep'=4,'shard'=8] {'rep'}, dimensions={0}, use_global_device_ids=true | all-gather | bytes 737280 | tf_op jit(solution)/shard_map/all_gather | solution.py:354
  451.5 1.0 copy.50
  452.5 0.9 bitcast_convert_fusion
  453.4 0.7 bitcast_convert_fusion.1
  (84 shorter events, 11.6 us)
Async XLA Ops:
  7.2 11.6 %copy-start = (bf16[169,16]{0,1:T(8,128)(2,1)S(1)}, bf16[169,16]{0,1:T(8,128)(2,1)}, u32[]{:S(2)}) copy-start(bf16[169,16]{0,1:T(8,128)(2,1)} %param.35) | copy-start | bytes 16228
  7.2 13.6 %copy-start.5 = (f32[4,64,64]{2,1,0:T(8,128)S(1)}, f32[4,64,64]{2,1,0:T(8,128)}, u32[]{:S(2)}) copy-start(f32[4,64,64]{2,1,0:T(8,128)} %constant.79) | copy-start | bytes 196612
  7.2 39.2 %all-gather.10.cloned.1.call-start = ((), (), s32[]{:S(2)}) async-start(), calls=%async_computation.6 | async-start | bytes 2211840 | tf_op jit(solution)/shard_map/all_gather | solution.py:266
  15.5 71.9 %all-gather.8.cloned.1.call-start = ((), (), s32[]{:S(2)}) async-start(), calls=%async_computation.3 | async-start | bytes 2359296 | tf_op jit(solution)/shard_map/all_gather | solution.py:270
  16.3 96.0 %all-gather.6.cloned.1.call-start = ((), (), s32[]{:S(2)}) async-start(), calls=%async_computation.2 | async-start | bytes 2949120 | tf_op jit(solution)/shard_map/all_gather | solution.py:267
  18.1 310.6 %reduce-scatter.3.cloned.1.call-start = ((), (), s32[]{:S(2)}) async-start(), calls=%async_computation.4 | async-start | bytes 1622016 | tf_op jit(solution)/shard_map/reduce_scatter | solution.py:381
  232.5 2.2 copy-start.2
  232.6 207.5 %reduce-scatter.5.cloned.1.call-start = ((), (), s32[]{:S(2)}) async-start(), calls=%async_computation.5 | async-start | bytes 4866048 | tf_op jit(solution)/shard_map/reduce_scatter | solution.py:353
  234.6 1.1 copy-start.3
  238.1 1.0 copy-start.4
  238.1 1.4 copy-start.15
  238.2 2.9 copy-start.13
  238.2 2.9 copy-start.14
  238.2 2.9 copy-start.10
  238.2 2.9 copy-start.6
  238.2 2.9 copy-start.9
  238.2 2.9 copy-start.12
  238.2 2.9 copy-start.11
  238.2 3.0 copy-start.8
  238.2 3.0 copy-start.7
  281.0 173.0 %copy-start.1 = (bf16[169,16]{0,1:T(8,128)(2,1)S(1)}, bf16[169,16]{0,1:T(8,128)(2,1)}, u32[]{:S(2)}) copy-start(bf16[169,16]{0,1:T(8,128)(2,1)} %param.35) | copy-start | bytes 16228
Sparse Core Ops, SparseCore 0:
  15.6 30.7 all-gather.9
  48.0 28.6 all-gather.7
  78.9 33.3 all-gather.5
  232.7 95.9 reduce-scatter.2
  334.0 106.0 reduce-scatter.4
